TPU v7x, 32 devices: a whole 2x2x4 slice. The times are simulated.
32 devices in a mesh: row: 8 (over y, x, core), col: 4 (over z).
Axes of the slice: x: 2, y: 2, z: 4, core: 2. Of those that a mesh axis runs over, the one named last changes fastest.
Arguments:
- perturbation: bfloat16 [16384, 16384], P('row', 'col'), may hold values from -0.046875 to 0.046875
- basis: bfloat16 [16384, 16384], P('row', 'col'), may hold values from -0.125 to 0.125
- orbitals: bfloat16 [16384, 512], P('col', 'row'), may hold values from -6 to 6
- pair_mask: int32 [16384, 512], P('col'), may hold values 0 or 1
- energies: float32 [16384], P('col'), may hold values from 1 to 4
- occ_energies: float32 [512], replicated, may hold values from -3 to -1
Outputs:
- response: float32 [16384, 512], P('row', 'col')
All inputs are finite; a program needn't handle non-finite values. No bound on the sum of `pair_mask` on one device may be relied on, other than what follows from the above.
Results may differ from a plain program's by a relative error of at most 0.0037.
Values may be sent and summed in bfloat16 or wider, within the bound.
A program may use at most 128 MiB of HBM per device.

v0:
```python
import jax
import jax.numpy as jnp
from jax import lax
from jax.sharding import PartitionSpec as P


def scaled(projection, mask_block, level_block, occ_block):
    spacing = level_block[:, None] - occ_block[None, :]
    return jnp.where(mask_block == 1, projection / spacing, jnp.zeros_like(projection)).astype(
        jnp.bfloat16
    )


def shards(perturbation, basis, orbitals, pair_mask, energies, occ_energies):
    partial_value = jnp.dot(
        perturbation,
        lax.all_gather(orbitals, "row", axis=1, tiled=True),
        preferred_element_type=jnp.float32,
    )
    share = lax.psum_scatter(partial_value, "col", scatter_dimension=1, tiled=True).astype(
        jnp.bfloat16
    )
    image = lax.all_gather(share, "col", axis=1, tiled=True)
    row_count = lax.axis_size("row")
    width = pair_mask.shape[1] // row_count
    first = lax.axis_index("row") * width
    project_part = jnp.dot(basis.T, image, preferred_element_type=jnp.float32)
    proj_share = lax.psum_scatter(project_part, "row", scatter_dimension=1, tiled=True)
    mask_block = lax.dynamic_slice_in_dim(pair_mask, first, width, 1)
    occ_block = lax.dynamic_slice_in_dim(occ_energies, first, width, 0)
    coef_share = scaled(proj_share, mask_block, energies, occ_block)
    rotated = jnp.dot(
        basis,
        lax.all_gather(coef_share, "row", axis=1, tiled=True),
        preferred_element_type=jnp.float32,
    )
    return lax.psum_scatter(rotated, "col", scatter_dimension=1, tiled=True)


def solution(mesh):
    return jax.shard_map(
        shards,
        mesh=mesh,
        in_specs=(P("row", "col"), P("row", "col"), P("col", "row"), P("col", None), P("col"), P()),
        out_specs=P("row", "col"),
        check_vma=False,
    )
```

profile of v0, /device:TPU:0, one launch (start us, length us, event | category | flops | bytes accessed | tf_op | source)
XLA Modules:
  0.0 415.0 jit_solution(2916585314646299638)
XLA Ops:
  6.5 0.0 all-gather.4.cloned.1.call-start
  6.5 0.7 all-gather.4.cloned.1.call-update
  7.3 0.0 reduce-scatter.6.cloned.1.call-start
  7.3 41.4 %all-gather.4.cloned.1.call-done = bf16[4096,512]{0,1:T(8,128)(2,1)} async-done(((bf16[4096,64]{0,1:T(8,128)(2,1)}), bf16[4096,512]{0,1:T(8,128)(2,1)}) %all-gather.4.cloned.1.call-update) | async-done | bytes 4194320 | tf_op jit(solution)/shard_map/all_gather | solution.py:17
  48.7 14.9 %fusion.2 = f32[2048,512]{1,0:T(8,128)} fusion(bf16[2048,4096]{1,0:T(8,128)(2,1)} %param.6, bf16[4096,512]{0,1:T(8,128)(2,1)} %all-gather.4.cloned.1.call-done), kind=kOutput, calls=%fused_computation.5 | convolution fusion | flops 8589934592 | bytes 25165824 | tf_op jit(solution)/shard_map/dot_general | solution.py:15
  63.6 0.0 reduce-scatter.6.cloned.1.call-update
  63.7 0.0 all-gather.6.cloned.1.call-start
  63.7 76.9 %reduce-scatter.6.cloned.1.call-done = f32[2048,128]{1,0:T(8,128)} async-done(((f32[2048,512]{1,0:T(8,128)}), f32[2048,128]{1,0:T(8,128)}) %reduce-scatter.6.cloned.1.call-update) | async-done | bytes 1048592 | tf_op jit(solution)/shard_map/reduce_scatter | solution.py:20
  140.6 2.1 convert_element_type.6
  142.7 0.0 all-gather.6.cloned.1.call-update
  142.7 0.0 reduce-scatter.10.cloned.1.call-start
  142.7 46.9 %all-gather.6.cloned.1.call-done = bf16[2048,512]{1,0:T(8,128)(2,1)} async-done(((bf16[2048,128]{1,0:T(8,128)(2,1)}), bf16[2048,512]{1,0:T(8,128)(2,1)}) %all-gather.6.cloned.1.call-update) | async-done | bytes 2097168 | tf_op jit(solution)/shard_map/all_gather | solution.py:23
  189.6 15.1 %fusion.3 = f32[512,4096]{1,0:T(8,128)} fusion(bf16[2048,512]{1,0:T(8,128)(2,1)} %all-gather.6.cloned.1.call-done, bf16[2048,4096]{1,0:T(8,128)(2,1)} %param.7), kind=kOutput, calls=%fused_computation.6 | convolution fusion | flops 8589934592 | bytes 27262976 | tf_op jit(solution)/shard_map/dot_general | solution.py:27
  204.7 0.0 reduce-scatter.10.cloned.1.call-update
  204.8 0.0 copy-start
  204.8 0.0 all-gather.8.cloned.1.call-start
  204.8 2.2 constant_dynamic-slice_fusion
  207.0 0.6 copy.16
  207.6 0.8 dynamic_slice.7
  208.4 66.1 %reduce-scatter.10.cloned.1.call-done = f32[64,4096]{1,0:T(8,128)} async-done(((f32[512,4096]{1,0:T(8,128)}), f32[64,4096]{1,0:T(8,128)}) %reduce-scatter.10.cloned.1.call-update) | async-done | bytes 1048592
  274.4 0.0 copy-done
  274.5 2.3 fusion.1
  276.7 0.0 all-gather.8.cloned.1.call-update
  276.7 0.2 reduce-scatter.8.cloned.1.call-start
  277.0 36.6 %all-gather.8.cloned.1.call-done = bf16[4096,512]{0,1:T(8,128)(2,1)} async-done(((bf16[4096,64]{0,1:T(8,128)(2,1)}), bf16[4096,512]{0,1:T(8,128)(2,1)}) %all-gather.8.cloned.1.call-update) | async-done | bytes 4194320 | tf_op jit(solution)/shard_map/all_gather | solution.py:34
  313.6 15.1 %convolution_bitcast_fusion = f32[2048,512]{0,1:T(8,128)} fusion(bf16[4096,512]{0,1:T(8,128)(2,1)} %all-gather.8.cloned.1.call-done, bf16[2048,4096]{1,0:T(8,128)(2,1)} %param.7), kind=kOutput, calls=%fused_computation | convolution fusion | flops 8589934592 | bytes 25165824 | tf_op jit(solution)/shard_map/dot_general | solution.py:32
  328.7 0.0 reduce-scatter.8.cloned.1.call-update
  328.7 76.9 %reduce-scatter.8.cloned.1.call-done = f32[2048,128]{0,1:T(8,128)} async-done(((f32[2048,512]{0,1:T(8,128)}), f32[2048,128]{0,1:T(8,128)}) %reduce-scatter.8.cloned.1.call-update) | async-done | bytes 1048592 | tf_op jit(solution)/shard_map/reduce_scatter | solution.py:37
  405.6 2.5 copy.13
Async XLA Ops:
  6.5 42.2 %all-gather.4.cloned.1.call-start = ((), (), s32[]{:S(2)}) async-start(), calls=%async_computation.3 | async-start | bytes 4718592 | tf_op jit(solution)/shard_map/all_gather | solution.py:17
  7.3 133.3 %reduce-scatter.6.cloned.1.call-start = ((), (), s32[]{:S(2)}) async-start(), calls=%async_computation.4 | async-start | bytes 5242880 | tf_op jit(solution)/shard_map/reduce_scatter | solution.py:20
  63.7 125.9 %all-gather.6.cloned.1.call-start = ((), (), s32[]{:S(2)}) async-start(), calls=%async_computation.5 | async-start | bytes 2621440 | tf_op jit(solution)/shard_map/all_gather | solution.py:23
  142.7 131.8 %reduce-scatter.10.cloned.1.call-start = ((), (), s32[]{:S(2)}) async-start(), calls=%async_computation.8 | async-start | bytes 9437184
  204.8 69.7 %copy-start = (f32[4096]{0:T(1024)S(1)}, f32[4096]{0:T(1024)}, u32[]{:S(2)}) copy-start(f32[4096]{0:T(1024)} %param.10) | copy-start | bytes 49156
  204.8 108.8 %all-gather.8.cloned.1.call-start = ((), (), s32[]{:S(2)}) async-start(), calls=%async_computation.6 | async-start | bytes 4718592 | tf_op jit(solution)/shard_map/all_gather | solution.py:34
  276.7 128.9 %reduce-scatter.8.cloned.1.call-start = ((), (), s32[]{:S(2)}) async-start(), calls=%async_computation.7 | async-start | bytes 5242880 | tf_op jit(solution)/shard_map/reduce_scatter | solution.py:37
Sparse Core Ops, SparseCore 0:
  9.2 39.4 all-gather.3
  63.8 76.7 reduce-scatter.5
  142.8 46.7 all-gather.5
  204.9 69.5 reduce-scatter.9
  276.9 36.6 all-gather.7
  328.8 76.7 reduce-scatter.7
where the time goes:
time: 415 us
  waiting for transfers between devices  346 us (83%)
  matrix products  45.1 us (11%)
  between operations  13.5 us (3%)
  local copies, waits for them, and re-layouts  6.09 us (1%)
  other arithmetic  4.34 us (1%)
    reduce_scatter x1, waiting for transfers between devices, shards(): return lax.psum_scatter(rotated, 'col', scatter_dimension=1, tiled=True)  76.9 us
    reduce_scatter x1, waiting for transfers between devices, shards(): lax.psum_scatter(partial_value, 'col', scatter_dimension=1, tiled=True)  76.9 us
    unnamed x7, waiting for transfers between devices  66.8 us
    all_gather x1, waiting for transfers between devices, shards(): image = lax.all_gather(share, 'col', axis=1, tiled=True)  46.9 us
    all_gather x1, waiting for transfers between devices, shards(): lax.all_gather(orbitals, 'row', axis=1, tiled=True)  41.4 us
    all_gather x1, waiting for transfers between devices, shards(): lax.all_gather(coef_share, 'row', axis=1, tiled=True)  36.6 us
    dot_general x1, matrix products, shards(): project_part = jnp.dot(basis.T, image, preferred_element_type=jnp.float32)  15.1 us
    dot_general x1, matrix products, shards(): jnp.dot(basis, lax.all_gather(coef_share, 'row', axis=1, tiled=True), pre...  15.1 us
  transfers between devices with their start and end apart: 6, of which 6 were waited for; matrix products, arithmetic and copies ran while one was open for 1% of the time, Pallas kernels for 0%

commit v1 on v0

v1 whole, which is shorter than its diff:
```python
import functools

import jax
import jax.numpy as jnp
from jax import lax
from jax.experimental import pallas as pl
from jax.experimental.pallas import tpu as pltpu
from jax.sharding import PartitionSpec as P

MESH = pl.DeviceIdType.MESH
F32, BF16 = jnp.float32, jnp.bfloat16
NT = (((1,), (1,)), ((), ()))


def plan(nr, nc, rows, cols, width):
    chunks = max(1, min(4, width // 16))
    unit = width // chunks
    tile = min(512, rows)
    bits = nr.bit_length() - 1
    assert 1 << bits == nr and nr % nc == 0
    return chunks, unit, tile, rows // tile, bits


def kernel(nr, nc, sizes, hop, fhop, gaps, x_hbm, p_hbm, b_hbm, w_ref, out_ref,
           xg, pt, bv, yown, lr, rr, ls, rs, img, proj, drecv, fp, fl, fr, fs,
           x_sem, p_sem, b_sem, ag_s, ag_r, d_s, d_r, l_s, l_r, r_s, r_r, f_s, fl_r, fr_r):
    chunks, unit, tile, tiles, bits = sizes
    rows, cols = bv.shape
    steps_b = chunks * tiles
    q = nr // nc
    me, z = lax.axis_index("row"), lax.axis_index("col")
    ring = yown.shape[0]

    def bit_values(odd):
        order = list(range(bits - 1, 0, -1)) if odd else list(range(1, bits))
        return [1 << b for b in order + [0]]

    even_bits, odd_bits = bit_values(False), bit_values(True)

    def place(d, odd):
        even_at = sum(((d // v) % 2) * (1 << t) for t, v in enumerate(even_bits))
        odd_at = sum(((d // v) % 2) * (1 << t) for t, v in enumerate(odd_bits))
        return jnp.where(odd == 1, odd_at, even_at)

    def peer(t, odd):
        ve, vo = even_bits[t], odd_bits[t]
        pe = me + (1 - 2 * ((me // ve) % 2)) * ve
        po = me + (1 - 2 * ((me // vo) % 2)) * vo
        return jnp.where(odd == 1, po, pe)

    def at_unit(u, n=1):
        return pl.ds(pl.multiple_of(u * unit, unit), n * unit)

    def gather_copy(which, k, t):
        odd = k % 2
        base = (place(me, odd) // (1 << t)) * (1 << t)
        block = xg.at[k, at_unit(base, 1 << t)]
        return pltpu.make_async_remote_copy(
            block, block, ag_s.at[which, k, t], ag_r.at[which, k, t],
            device_id=(peer(t, odd), z), device_id_type=MESH)

    def halves(k, t):
        at = place(me, k % 2)
        base = (at // (2 << t)) * (2 << t)
        bit = (at // (1 << t)) % 2
        return base + bit * (1 << t), base + (1 - bit) * (1 << t)

    def reduce_copy(k, t):
        _, away = halves(k, t)
        return pltpu.make_async_remote_copy(
            proj.at[k % 2, at_unit(away, 1 << t)],
            drecv.at[k, pl.ds(((1 << t) - 1) * unit, (1 << t) * unit)],
            d_s.at[k, t], d_r.at[k, t], device_id=(peer(t, k % 2), z), device_id_type=MESH)

    def right_copy(j):
        return pltpu.make_async_remote_copy(
            rs.at[j], lr.at[j], r_s.at[j], l_r.at[j], device_id=(me, jnp.minimum(z + 1, nc - 1)), device_id_type=MESH)

    def left_copy(j):
        return pltpu.make_async_remote_copy(
            ls.at[j], rr.at[j], l_s.at[j], r_r.at[j], device_id=(me, jnp.maximum(z - 1, 0)), device_id_type=MESH)

    def f_right(k, c):
        return pltpu.make_async_remote_copy(
            fs.at[k, c], fl.at[k, c], f_s.at[k, c], fl_r.at[k, c],
            device_id=(me, jnp.minimum(z + 1, nc - 1)), device_id_type=MESH)

    def f_left(k, c):
        return pltpu.make_async_remote_copy(
            fs.at[k, c], fr.at[k, c], f_s.at[k, c], fr_r.at[k, c],
            device_id=(me, jnp.maximum(z - 1, 0)), device_id_type=MESH)

    def p_copy(s):
        return pltpu.make_async_copy(
            p_hbm.at[pl.ds(pl.multiple_of((s % tiles) * tile, tile), tile)], pt.at[s % 2], p_sem.at[s % 2])

    def x_copy(k):
        return pltpu.make_async_copy(
            x_hbm.at[pl.ds(k * unit, unit)], xg.at[k, at_unit(place(me, k % 2))], x_sem.at[k])

    b_copy = pltpu.make_async_copy(b_hbm, bv, b_sem)

    for k in range(chunks):
        x_copy(k).start()
    p_copy(0).start()

    barrier = pltpu.get_barrier_semaphore()
    for b in range(bits):
        other = me + (1 - 2 * ((me // (1 << b)) % 2)) * (1 << b)
        pl.semaphore_signal(barrier, inc=1, device_id=(other, z), device_id_type=MESH)

    @pl.when(z > 0)
    def _():
        pl.semaphore_signal(barrier, inc=1, device_id=(me, jnp.maximum(z - 1, 0)), device_id_type=MESH)

    @pl.when(z < nc - 1)
    def _():
        pl.semaphore_signal(barrier, inc=1, device_id=(me, jnp.minimum(z + 1, nc - 1)), device_id_type=MESH)

    pl.semaphore_wait(barrier, bits + jnp.minimum(z, 1) + jnp.minimum(nc - 1 - z, 1))

    for k in range(chunks):
        x_copy(k).wait()
        gather_copy(0, k, 0).start()
    b_copy.start()

    def gather_step(which, k, t):
        gather_copy(which, k, t).wait()
        if t + 1 < bits:
            gather_copy(which, k, t + 1).start()

    for t in range(bits):
        gather_step(0, 0, t)

    def image_tile(s):
        p_copy(s).wait()

        @pl.when(s + 1 < steps_b)
        def _():
            p_copy(s + 1).start()

        yown[s % ring] = lax.dot_general(xg[s // tiles], pt[s % 2], NT, preferred_element_type=F32)

    def pass_right(j):
        @pl.when(z == 0)
        def _():
            rs[j] = yown[j % ring].astype(BF16)

        @pl.when(z > 0)
        def _():
            right_copy(j).wait_recv()

        @pl.when(jnp.logical_and(z > 0, z < nc - 1))
        def _():
            rs[j] = (yown[j % ring] + lr[j].astype(F32)).astype(BF16)

        @pl.when(z < nc - 1)
        def _():
            right_copy(j).start()

    def pass_left(j):
        @pl.when(z == nc - 1)
        def _():
            ls[j] = yown[j % ring].astype(BF16)

        @pl.when(z < nc - 1)
        def _():
            left_copy(j).wait_recv()

        @pl.when(jnp.logical_and(z > 0, z < nc - 1))
        def _():
            ls[j] = (yown[j % ring] + rr[j].astype(F32)).astype(BF16)

        @pl.when(z > 0)
        def _():
            left_copy(j).start()

    def image_done(j):
        @pl.when(z > 0)
        def _():
            yown[j % ring] += lr[j].astype(F32)

        @pl.when(z < nc - 1)
        def _():
            yown[j % ring] += rr[j].astype(F32)

        k, t = j // tiles, j % tiles
        img[k % 2, :, pl.ds(pl.multiple_of(t * tile, tile), tile)] = yown[j % ring].astype(BF16)

    ctile = min(512, cols)

    def project(k):
        @pl.when(k == 0)
        def _():
            b_copy.wait()

        def body(i, carry):
            at = pl.ds(pl.multiple_of(i * ctile, ctile), ctile)
            proj[k % 2, :, at] = jnp.dot(img[k % 2], bv[:, at], preferred_element_type=F32)
            return carry

        lax.fori_loop(0, cols // ctile, body, 0)
        reduce_copy(k, bits - 1).start()

    def reduce_step(k, t):
        reduce_copy(k, t).wait()
        keep, _ = halves(k, t)
        at = at_unit(keep, 1 << t)
        got = drecv[k, pl.ds(((1 << t) - 1) * unit, (1 << t) * unit)]
        if t > 0:
            proj[k % 2, at] += got
            reduce_copy(k, t - 1).start()
        else:
            coef = (proj[k % 2, at] + got) * w_ref[pl.ds(pl.multiple_of(k * unit, unit), unit)]
            xg[k, at] = coef.astype(BF16)
            gather_copy(1, k, 0).start()

    def respond(k):
        def body(i, carry):
            at = pl.ds(pl.multiple_of(i * tile, tile), tile)
            fp[k % 2, :, at] = lax.dot_general(xg[k], bv[at], NT, preferred_element_type=F32)
            return carry

        lax.fori_loop(0, rows // tile, body, 0)

    def share(k, c, i):
        return fp[k % 2, at_unit(place(c * q + i, k % 2))]

    def out_right(k):
        for c in range(nc - 1, 0, -1):
            @pl.when(jnp.logical_and(z == 0, c > z))
            def _():
                for i in range(q):
                    fs[k, c, i * unit:(i + 1) * unit] = share(k, c, i).astype(BF16)

            @pl.when(jnp.logical_and(z > 0, c > z))
            def _():
                f_right(k, c).wait_recv()
                for i in range(q):
                    at = slice(i * unit, (i + 1) * unit)
                    fs[k, c, at] = (share(k, c, i) + fl[k, c, at].astype(F32)).astype(BF16)

            @pl.when(c > z)
            def _():
                f_right(k, c).start()

    def out_left(k):
        for c in range(nc - 1):
            @pl.when(jnp.logical_and(z == nc - 1, c < z))
            def _():
                for i in range(q):
                    fs[k, c, i * unit:(i + 1) * unit] = share(k, c, i).astype(BF16)

            @pl.when(jnp.logical_and(z < nc - 1, c < z))
            def _():
                f_left(k, c).wait_recv()
                for i in range(q):
                    at = slice(i * unit, (i + 1) * unit)
                    fs[k, c, at] = (share(k, c, i) + fr[k, c, at].astype(F32)).astype(BF16)

            @pl.when(c < z)
            def _():
                f_left(k, c).start()

    def out_done(k):
        for i in range(q):
            out_ref[k, i] = share(k, z, i)

        @pl.when(z > 0)
        def _():
            f_right(k, z).wait_recv()
            for i in range(q):
                out_ref[k, i] += fl[k, z, i * unit:(i + 1) * unit].astype(F32)

        @pl.when(z < nc - 1)
        def _():
            f_left(k, z).wait_recv()
            for i in range(q):
                out_ref[k, i] += fr[k, z, i * unit:(i + 1) * unit].astype(F32)

    def each(s, offset, task):
        d = s - offset
        k = d // tiles

        @pl.when(jnp.logical_and(d >= 0, jnp.logical_and(d % tiles == 0, k < chunks)))
        def _():
            task(k)

    def tile_task(s, lag, task):
        j = s - lag

        @pl.when(jnp.logical_and(j >= 0, j < steps_b))
        def _():
            task(j)

    reduce_gaps, gather_gaps = gaps
    at_project = tiles - 1 + hop * (nc - 1)
    timeline, now = [], at_project
    for n, t in enumerate(range(bits - 1, -1, -1)):
        now += reduce_gaps[min(n, len(reduce_gaps) - 1)]
        timeline.append((now, functools.partial(lambda t, k: reduce_step(k, t), t)))
    for t in range(bits):
        now += gather_gaps[min(t, len(gather_gaps) - 1)]
        timeline.append((now, functools.partial(lambda t, k: gather_step(1, k, t), t)))
    at_respond = now
    last = (chunks - 1) * tiles + at_respond + fhop * (nc - 1) + 1

    def step(s, carry):
        tile_task(s, 0, image_tile)
        tile_task(s, hop * z, pass_right)
        tile_task(s, hop * (nc - 1 - z), pass_left)
        tile_task(s, hop * (nc - 1), image_done)
        if chunks > 1:
            for t in range(bits):
                ahead = min(1 + t, tiles - 1)
                d = s - ahead
                k = d // tiles + 1

                @pl.when(jnp.logical_and(d >= 0, jnp.logical_and(d % tiles == 0, k < chunks)))
                def _():
                    gather_step(0, k, t)
        for offset, task in timeline:
            each(s, offset, task)
        each(s, at_project, project)
        each(s, at_respond, respond)
        each(s, at_respond + fhop * z, out_right)
        each(s, at_respond + fhop * (nc - 1 - z), out_left)
        each(s, at_respond + fhop * (nc - 1), out_done)
        return carry

    lax.fori_loop(0, last, step, 0)

    def drain(j, carry):
        @pl.when(z < nc - 1)
        def _():
            right_copy(j).wait_send()

        @pl.when(z > 0)
        def _():
            left_copy(j).wait_send()

        return carry

    lax.fori_loop(0, steps_b, drain, 0)

    def drain_out(k, carry):
        for c in range(nc):
            @pl.when(c > z)
            def _():
                f_right(k, c).wait_send()

            @pl.when(c < z)
            def _():
                f_left(k, c).wait_send()

        return carry

    lax.fori_loop(0, chunks, drain_out, 0)


def shards(perturbation, basis, orbitals, pair_mask, energies, occ_energies):
    nr, nc = lax.axis_size("row"), lax.axis_size("col")
    rows, cols = perturbation.shape
    width = orbitals.shape[1]
    sizes = plan(nr, nc, rows, cols, width)
    chunks, unit, tile, tiles, bits = sizes
    q = nr // nc
    count = nr * unit
    hop, fhop, gaps = 2, 2, ((1, 4, 2), (1, 2, 1))
    ring = hop * (nc - 1) + 1
    n = chunks * tiles

    first = lax.axis_index("row") * width
    mask_block = lax.dynamic_slice_in_dim(pair_mask, first, width, 1).T
    occ_block = lax.dynamic_slice_in_dim(occ_energies, first, width, 0)
    inverse = jnp.where(mask_block == 1, 1.0 / (energies[None, :] - occ_block[:, None]), 0.0)

    dma = pltpu.SemaphoreType.DMA
    result = pl.pallas_call(
        functools.partial(kernel, nr, nc, sizes, hop, fhop, gaps),
        out_shape=jax.ShapeDtypeStruct((chunks, q, unit, rows), F32),
        in_specs=[pl.BlockSpec(memory_space=pl.ANY)] * 3 + [pl.BlockSpec(memory_space=pltpu.VMEM)],
        out_specs=pl.BlockSpec(memory_space=pltpu.VMEM),
        scratch_shapes=[
            pltpu.VMEM((chunks, count, cols), BF16),
            pltpu.VMEM((2, tile, cols), BF16),
            pltpu.VMEM((rows, cols), BF16),
            pltpu.VMEM((ring, count, tile), F32),
            pltpu.VMEM((n, count, tile), BF16),
            pltpu.VMEM((n, count, tile), BF16),
            pltpu.VMEM((n, count, tile), BF16),
            pltpu.VMEM((n, count, tile), BF16),
            pltpu.VMEM((2, count, rows), BF16),
            pltpu.VMEM((2, count, cols), F32),
            pltpu.VMEM((chunks, (nr - 1) * unit, cols), F32),
            pltpu.VMEM((2, count, rows), F32),
            pltpu.VMEM((chunks, nc, q * unit, rows), BF16),
            pltpu.VMEM((chunks, nc, q * unit, rows), BF16),
            pltpu.VMEM((chunks, nc, q * unit, rows), BF16),
            dma((chunks,)), dma((2,)), dma,
            dma((2, chunks, bits)), dma((2, chunks, bits)),
            dma((chunks, bits)), dma((chunks, bits)),
            dma((n,)), dma((n,)), dma((n,)), dma((n,)),
            dma((chunks, nc)), dma((chunks, nc)), dma((chunks, nc)),
        ],
        compiler_params=pltpu.CompilerParams(
            collective_id=0, has_side_effects=True, vmem_limit_bytes=63 * 1024 * 1024),
    )(orbitals.T, perturbation, basis, inverse)
    return result.transpose(3, 1, 0, 2).reshape(rows, q * width)


def solution(mesh):
    return jax.shard_map(
        shards,
        mesh=mesh,
        in_specs=(P("row", "col"), P("row", "col"), P("col", "row"), P("col", None), P("col"), P()),
        out_specs=P("row", "col"),
        check_vma=False,
    )
```

time: 415 us -> 218 us (0.53)
  waiting for transfers between devices: 346 us -> 0 us
  Pallas kernels: 0 us -> 210 us
  matrix products: 45.1 us -> 0 us
  between operations: 13.5 us -> 0.03 us
    pallas_call x0 -> x1, Pallas kernels: none -> 210 us  [shards(): pl.pallas_call(functools.partial(kernel, nr, nc, sizes, hop, fhop, gaps),...]
    reduce_scatter x2 -> x0, waiting for transfers between devices: 154 us -> none  [the longest x1 76.9 us: shards(): return lax.psum_scatter(rotated, 'col', scatter_dimension=1, tiled=True)]
    all_gather x3 -> x0, waiting for transfers between devices: 125 us -> none  [the longest x1 46.9 us: shards(): image = lax.all_gather(share, 'col', axis=1, tiled=True)]
    unnamed x7 -> x0, waiting for transfers between devices: 66.8 us -> none
    dot_general x3 -> x0, matrix products: 45.1 us -> none  [the longest x1 15.1 us: shards(): project_part = jnp.dot(basis.T, image, preferred_element_type=jnp.float32)]
    convert_element_type x2 -> x0, other arithmetic: 4.34 us -> none  [the longest x1 2.27 us: scaled(): jnp.where(mask_block == 1, projection / spacing, jnp.zeros_like(projection))]
  transfers between devices with their start and end apart: 6 -> 0, of which waited for: 6 -> 0; matrix products, arithmetic and copies ran while one was open for 1% -> 0% of each run, Pallas kernels for 0% -> 0%
where the time goes in v1:
time: 218 us
  Pallas kernels  210 us (96%)
  local copies, waits for them, and re-layouts  6.13 us (3%)
    pallas_call x1, Pallas kernels, shards(): pl.pallas_call(functools.partial(kernel, nr, nc, sizes, hop, fhop, gaps),...  210 us

profile of v1, /device:TPU:0, one launch (start us, length us, event | category | flops | bytes accessed | tf_op | source)
XLA Modules:
  0.0 217.6 jit_solution(1778029882007796064)
XLA Ops:
  0.0 0.8 dynamic_slice.7
  0.8 2.2 %constant_dynamic-slice_fusion = s32[4096,64]{1,0:T(8,128)S(1)} fusion(s32[4096,512]{1,0:T(8,128)} %param.9, s32[]{:T(128)S(6)} %select_n.8), kind=kLoop, calls=%fused_computation.1 | loop fusion | bytes 2097156 | tf_op jit(solution)/shard_map/dynamic_slice | solution.py:374
  2.9 0.6 copy.11
  3.5 1.9 divide_select_fusion.w_ref
  5.4 209.6 %shard_map.64 = f32[4,2,16,2048]{3,2,1,0:T(8,128)} custom-call(bf16[64,4096]{1,0:T(8,128)(2,1)} %bitcast.7, bf16[2048,4096]{1,0:T(8,128)(2,1)} %p_hbm.1, bf16[2048,4096]{1,0:T(8,128)(2,1)} %b_hbm.1, f32[64,4096]{1,0:T(8,128)} %divide_select_fusion.w_ref), custom_call_target="tpu_custom_call" | custom-call | tf_op jit(solution)/shard_map/pallas_call | solution.py:379
  215.0 1.3 copy.9
  216.3 1.3 copy.10

commit v2 on v1

--- a/solution.py
+++ b/solution.py
@@ -366,7 +366,7 @@
     chunks, unit, tile, tiles, bits = sizes
     q = nr // nc
     count = nr * unit
-    hop, fhop, gaps = 2, 2, ((1, 4, 2), (1, 2, 1))
+    hop, fhop, gaps = 1, 1, ((1, 2, 1), (1, 1, 1))
     ring = hop * (nc - 1) + 1
     n = chunks * tiles
 

time: 218 us -> 206 us (0.945)
  Pallas kernels: 210 us -> 197 us
    pallas_call x1, Pallas kernels: 210 us -> 197 us  [shards(): pl.pallas_call(functools.partial(kernel, nr, nc, sizes, hop, fhop, gaps),...]
where the time goes in v2:
time: 206 us
  Pallas kernels  197 us (96%)
  local copies, waits for them, and re-layouts  6.13 us (3%)
    pallas_call x1, Pallas kernels, shards(): pl.pallas_call(functools.partial(kernel, nr, nc, sizes, hop, fhop, gaps),...  197 us

profile of v2, /device:TPU:0, one launch (start us, length us, event | category | flops | bytes accessed | tf_op | source)
XLA Modules:
  0.0 205.5 jit_solution(1084044568611996342)
XLA Ops:
  0.0 0.8 dynamic_slice.7
  0.8 2.2 %constant_dynamic-slice_fusion = s32[4096,64]{1,0:T(8,128)S(1)} fusion(s32[4096,512]{1,0:T(8,128)} %param.9, s32[]{:T(128)S(6)} %select_n.8), kind=kLoop, calls=%fused_computation.1 | loop fusion | bytes 2097156 | tf_op jit(solution)/shard_map/dynamic_slice | solution.py:374
  2.9 0.6 copy.11
  3.5 1.9 divide_select_fusion.w_ref
  5.4 197.5 %shard_map.64 = f32[4,2,16,2048]{3,2,1,0:T(8,128)} custom-call(bf16[64,4096]{1,0:T(8,128)(2,1)} %bitcast.7, bf16[2048,4096]{1,0:T(8,128)(2,1)} %p_hbm.1, bf16[2048,4096]{1,0:T(8,128)(2,1)} %b_hbm.1, f32[64,4096]{1,0:T(8,128)} %divide_select_fusion.w_ref), custom_call_target="tpu_custom_call" | custom-call | tf_op jit(solution)/shard_map/pallas_call | solution.py:379
  202.9 1.3 copy.9
  204.2 1.3 copy.10
